TPU v7x, 32 devices: a whole 2x2x4 slice. The times are simulated.
32 devices in a mesh: row: 2 (over x), col: 4 (over y, core), depth: 4 (over z).
Axes of the slice: x: 2, y: 2, z: 4, core: 2. Of those that a mesh axis runs over, the one named last changes fastest.
Arguments:
- tokens: bfloat16 [1024, 8192], P(('row', 'col'), 'depth'), may hold values from -6 to 6
- gate_weight: bfloat16 [8192, 14336], P(('depth', 'row'), 'col'), may hold values from -0.0625 to 0.0625
- up_weight: bfloat16 [8192, 14336], P(('depth', 'row'), 'col'), may hold values from -0.0625 to 0.0625
- down_weight: bfloat16 [14336, 8192], P(('col', 'row'), 'depth'), may hold values from -0.125 to 0.125
- gate_keep: int32 [64, 112], replicated, may hold values from 0 to 1, as said below
- up_keep: int32 [64, 112], replicated, may hold values from 0 to 1, as said below
- down_keep: int32 [112, 64], replicated, may hold values from 0 to 1, as said below
Outputs:
- mixed: bfloat16 [1024, 8192], P(('row', 'col'), 'depth')
Inputs may be any that keep to these rules, and one draw needn't show every extreme that they name: `gate_keep`: 1 marks a kept block of the gate projection, 0 a dropped one. `up_keep`: 1 marks a kept block of the up projection, 0 a dropped one. `down_keep`: 1 marks a kept block of the down projection, 0 a dropped one.
All inputs are finite; a program needn't handle non-finite values.
Results may differ from a plain program's by a relative error of at most 0.005.
Values may be sent and summed in bfloat16 or wider, within the bound.
A program may use at most 128 MiB of HBM per device.

v0:
```python
import jax
import jax.numpy as jnp
from jax import lax
from jax.sharding import PartitionSpec as P

BLOCK = 128


def keep_table(keep, row_start, col_start, row_count, col_count):
    keep_bits = keep.astype(jnp.bfloat16)
    row_ids = (row_start + jnp.arange(row_count, dtype=jnp.int32)) // BLOCK
    col_ids = (col_start + jnp.arange(col_count, dtype=jnp.int32)) // BLOCK
    pick_rows = (row_ids[:, None] == jnp.arange(keep.shape[0], dtype=jnp.int32)[None, :]).astype(
        jnp.bfloat16
    )
    pick_cols = (jnp.arange(keep.shape[1], dtype=jnp.int32)[:, None] == col_ids[None, :]).astype(
        jnp.bfloat16
    )
    inner = jnp.dot(keep_bits, pick_cols, preferred_element_type=jnp.float32).astype(jnp.bfloat16)
    return jnp.dot(pick_rows, inner, preferred_element_type=jnp.float32).astype(jnp.bfloat16)


def add_panel(token_block, piece):
    return jnp.dot(token_block, piece, preferred_element_type=jnp.float32)


def on_device(tokens, gate_weight, up_weight, down_weight, gate_keep, up_keep, down_keep):
    depth_pos = lax.axis_index("depth")
    row_pos = lax.axis_index("row")
    column_pos = lax.axis_index("col")
    row_total = lax.axis_size("row")
    feature_rows = gate_weight.shape[0]
    hidden_cols = gate_weight.shape[1]
    feature_start = (depth_pos * row_total + row_pos) * feature_rows
    hidden_start = column_pos * hidden_cols
    gate_masked = gate_weight * keep_table(
        gate_keep, feature_start, hidden_start, feature_rows, hidden_cols
    )
    up_masked = up_weight * keep_table(
        up_keep, feature_start, hidden_start, feature_rows, hidden_cols
    )
    down_rows_count = down_weight.shape[0]
    down_features = down_weight.shape[1]
    down_start = (column_pos * row_total + row_pos) * down_rows_count
    down_masked = down_weight * keep_table(
        down_keep, down_start, depth_pos * down_features, down_rows_count, down_features
    )
    token_block = lax.all_gather(tokens, "col", axis=0, tiled=True)

    def add_one(piece):
        return add_panel(token_block, piece)

    gate = add_one(lax.all_gather(gate_masked, "row", axis=0, tiled=True))
    up = add_one(lax.all_gather(up_masked, "row", axis=0, tiled=True))
    both = jnp.stack((gate, up), 0)
    total = lax.psum(both, "depth")
    hidden = (jax.nn.silu(total[0]) * total[1]).astype(jnp.bfloat16)
    down_block = lax.all_gather(down_masked, "row", axis=0, tiled=True)
    mixed = lax.psum_scatter(
        jnp.dot(hidden, down_block, preferred_element_type=jnp.float32),
        "col",
        scatter_dimension=0,
        tiled=True,
    )
    return mixed.astype(jnp.bfloat16)


def solution(mesh):
    placed = (
        P(("row", "col"), "depth"),
        P(("depth", "row"), "col"),
        P(("depth", "row"), "col"),
        P(("col", "row"), "depth"),
        P(),
        P(),
        P(),
    )
    return jax.shard_map(
        on_device, mesh=mesh, in_specs=placed, out_specs=P(("row", "col"), "depth"), check_vma=False
    )
```

profile of v0, /device:TPU:0, one launch (start us, length us, event | category | flops | bytes accessed | tf_op | source)
XLA Modules:
  0.0 1130.8 jit_solution(13736283952018054441)
XLA Ops:
  6.5 0.0 all-gather.7.cloned.1.call-start
  6.5 0.7 all-gather.7.cloned.1.call-update
  7.3 0.0 all-gather.9.cloned.1.call-start
  7.4 7.0 fusion.3
  14.3 0.0 copy-start
  14.3 0.0 all-gather.9.cloned.1.call-update
  14.4 0.0 all-gather.5.cloned.1.call-start
  14.4 0.7 copy-done
  15.1 7.0 fusion.2
  22.1 0.0 copy-start.1
  22.1 0.0 all-gather.5.cloned.1.call-update
  22.1 0.0 all-gather.11.cloned.1.call-start
  22.2 0.6 copy-done.1
  22.8 7.1 fusion.4
  29.9 0.0 all-gather.11.cloned.1.call-update
  29.9 0.2 all-reduce.2.cloned.1.call-start
  30.2 4.1 all-gather.7.cloned.1.call-done
  34.2 0.0 copy-start.2
  34.2 177.1 %all-gather.9.cloned.1.call-done = bf16[2048,3584]{1,0:T(8,128)(2,1)} async-done(((bf16[1024,3584]{1,0:T(8,128)(2,1)}), bf16[2048,3584]{1,0:T(8,128)(2,1)}) %all-gather.9.cloned.1.call-update) | async-done | bytes 14680080 | tf_op jit(solution)/shard_map/all_gather | solution.py:54
  211.4 14.1 %convolution_bitcast_fusion = f32[1,512,3584]{1,2,0:T(8,128)} fusion(bf16[2048,3584]{1,0:T(8,128)(2,1)} %all-gather.9.cloned.1.call-done, bf16[512,2048]{1,0:T(8,128)(2,1)} %all-gather.7.cloned.1.call-done), kind=kOutput, calls=%fused_computation.11 | convolution fusion | flops 7516192768 | bytes 24117248 | tf_op jit(solution)/shard_map/dot_general | solution.py:24
  225.4 163.1 %all-gather.5.cloned.1.call-done = bf16[2048,3584]{1,0:T(8,128)(2,1)} async-done(((bf16[1024,3584]{1,0:T(8,128)(2,1)}), bf16[2048,3584]{1,0:T(8,128)(2,1)}) %all-gather.5.cloned.1.call-update) | async-done | bytes 14680080 | tf_op jit(solution)/shard_map/all_gather | solution.py:53
  388.5 0.0 copy-done.2
  388.5 13.5 %convolution_bitcast_fusion.1 = f32[1,512,3584]{1,2,0:T(8,128)} fusion(bf16[2048,3584]{1,0:T(8,128)(2,1)} %all-gather.5.cloned.1.call-done, bf16[512,2048]{1,0:T(8,128)(2,1)S(1)} %copy-done.2), kind=kOutput, calls=%fused_computation.12 | convolution fusion | flops 7516192768 | bytes 24117248 | tf_op jit(solution)/shard_map/dot_general | solution.py:24
  402.0 15.1 %pad_maximum_fusion = f32[2,512,3584]{1,2,0:T(8,128)} fusion(f32[1,512,3584]{1,2,0:T(8,128)} %convolution_bitcast_fusion, f32[1,512,3584]{1,2,0:T(8,128)} %convolution_bitcast_fusion.1), kind=kLoop, calls=%fused_computation | loop fusion | flops 3670016 | bytes 29360128 | tf_op jit(solution)/shard_map/stack | solution.py:55
  417.1 0.0 all-reduce.2.cloned.1.call-update
  417.2 0.3 reduce-scatter.2.cloned.1.call-start
  417.4 148.0 %all-gather.11.cloned.1.call-done = bf16[3584,2048]{1,0:T(8,128)(2,1)} async-done(((bf16[1792,2048]{1,0:T(8,128)(2,1)}), bf16[3584,2048]{1,0:T(8,128)(2,1)}) %all-gather.11.cloned.1.call-update) | async-done | bytes 14680080 | tf_op jit(solution)/shard_map/all_gather | solution.py:58
  565.5 496.1 %all-reduce.2.cloned.1.call-done = f32[2,512,3584]{1,2,0:T(8,128)} async-done(((f32[2,512,3584]{1,2,0:T(8,128)}), f32[2,512,3584]{1,2,0:T(8,128)}) %all-reduce.2.cloned.1.call-update) | async-done | bytes 14680080 | tf_op jit(solution)/shard_map/psum | solution.py:56
  1061.6 16.7 %fusion.5 = f32[512,2048]{1,0:T(8,128)} fusion(bf16[3584,2048]{1,0:T(8,128)(2,1)} %all-gather.11.cloned.1.call-done, f32[2,512,3584]{1,2,0:T(8,128)} %all-reduce.2.cloned.1.call-done), kind=kOutput, calls=%fused_computation.15 | convolution fusion | flops 7527202816 | bytes 33554432 | tf_op jit(solution)/shard_map/dot_general | solution.py:60
  1078.3 0.0 reduce-scatter.2.cloned.1.call-update
  1078.3 43.5 %reduce-scatter.2.cloned.1.call-done = f32[128,2048]{1,0:T(8,128)} async-done(((f32[512,2048]{1,0:T(8,128)}), f32[128,2048]{1,0:T(8,128)}) %reduce-scatter.2.cloned.1.call-update) | async-done | bytes 1048592 | tf_op jit(solution)/shard_map/reduce_scatter | solution.py:59
  1121.8 2.1 convert_element_type.52
  (4 shorter events, 0.1 us)
Async XLA Ops:
  6.5 27.7 %all-gather.7.cloned.1.call-start = ((), (), s32[]{:S(2)}) async-start(), calls=%async_computation.2 | async-start | bytes 2621440 | tf_op jit(solution)/shard_map/all_gather | solution.py:48
  7.3 204.1 %all-gather.9.cloned.1.call-start = ((), (), s32[]{:S(2)}) async-start(), calls=%async_computation.3 | async-start | bytes 22020096 | tf_op jit(solution)/shard_map/all_gather | solution.py:54
  14.3 0.8 copy-start
  14.4 374.1 %all-gather.5.cloned.1.call-start = ((), (), s32[]{:S(2)}) async-start(), calls=%async_computation.1 | async-start | bytes 22020096 | tf_op jit(solution)/shard_map/all_gather | solution.py:53
  22.1 0.8 copy-start.1
  22.1 543.4 %all-gather.11.cloned.1.call-start = ((), (), s32[]{:S(2)}) async-start(), calls=%async_computation.5 | async-start | bytes 22020096 | tf_op jit(solution)/shard_map/all_gather | solution.py:58
  29.9 1031.6 %all-reduce.2.cloned.1.call-start = ((), (), s32[]{:S(2)}) async-start(), calls=%async_computation.4 | async-start | bytes 29360128 | tf_op jit(solution)/shard_map/psum | solution.py:56
  34.2 354.2 %copy-start.2 = (bf16[512,2048]{1,0:T(8,128)(2,1)S(1)}, bf16[512,2048]{1,0:T(8,128)(2,1)}, u32[]{:S(2)}) copy-start(bf16[512,2048]{1,0:T(8,128)(2,1)} %all-gather.7.cloned.1.call-done) | copy-start | bytes 6291460
  417.2 704.7 %reduce-scatter.2.cloned.1.call-start = ((), (), s32[]{:S(2)}) async-start(), calls=%async_computation.6 | async-start | bytes 5242880 | tf_op jit(solution)/shard_map/reduce_scatter | solution.py:59
Sparse Core Ops, SparseCore 0:
  8.9 25.2 all-gather.6
  35.8 175.5 all-gather.8
  212.9 175.5 all-gather.4
  389.9 175.5 all-gather.10
  567.8 493.7 all-reduce.1
  1078.4 43.3 reduce-scatter.1
where the time goes:
time: 1130 us
  waiting for transfers between devices  1030 us (91%)
  matrix products  65.3 us (6%)
  other arithmetic  17.3 us (2%)
  between operations  13.5 us (1%)
    psum x1, waiting for transfers between devices, on_device(): total = lax.psum(both, 'depth')  496 us
    all_gather x1, waiting for transfers between devices, on_device(): up = add_one(lax.all_gather(up_masked, 'row', axis=0, tiled=True))  177 us
    all_gather x1, waiting for transfers between devices, on_device(): gate = add_one(lax.all_gather(gate_masked, 'row', axis=0, tiled=True))  163 us
    all_gather x1, waiting for transfers between devices, on_device(): down_block = lax.all_gather(down_masked, 'row', axis=0, tiled=True)  148 us
    reduce_scatter x1, waiting for transfers between devices, on_device(): lax.psum_scatter(jnp.dot(hidden, down_block, preferred_element_type=jnp.f...  43.5 us
    dot_general x2, matrix products, add_panel(): return jnp.dot(token_block, piece, preferred_element_type=jnp.float32)  27.6 us
  transfers between devices with their start and end apart: 6, of which 6 were waited for; matrix products, arithmetic and copies ran while one was open for 6% of the time, Pallas kernels for 0%

commit v1 on v0

v1 whole, which is shorter than its diff:
```python
import functools

import jax
import jax.numpy as jnp
from jax import lax
from jax.experimental import pallas as pl
from jax.experimental.pallas import tpu as pltpu
from jax.sharding import PartitionSpec as P

BLOCK = 128
CHUNK = 256
AHEAD = 3
MESH = pl.DeviceIdType.MESH
BF16 = jnp.bfloat16
F32 = jnp.float32


def layer_kernel(
    Z, tok, gate, up, down, gate_keep, up_keep, down_keep, mixed,
    w_recv, w_own, w_mask, d_own, d_mask, part, stage, recv, hid,
    x_ss, x_rs, own_sem, d_sem, r_ss, r_rs, g_ss, g_rs,
):
    z, r, c = lax.axis_index("depth"), lax.axis_index("row"), lax.axis_index("col")
    K = w_recv.shape[0]
    rows = gate.shape[0]
    units = gate.shape[1] // 2
    shard = part.shape[2]
    features = down.shape[1]
    row_blocks = rows // BLOCK
    unit_block = (c * 2 + r) * (units // BLOCK)
    has_right, has_left = z < Z - 1, z > 0
    mirror = Z - 1 - z

    barrier = pltpu.get_barrier_semaphore()
    pl.semaphore_signal(barrier, inc=1, device_id={"row": 1 - r}, device_id_type=MESH)

    @pl.when(has_right)
    def _():
        pl.semaphore_signal(barrier, inc=1, device_id={"depth": z + 1}, device_id_type=MESH)

    @pl.when(has_left)
    def _():
        pl.semaphore_signal(barrier, inc=1, device_id={"depth": z - 1}, device_id_type=MESH)

    pl.semaphore_wait(barrier, 1 + has_right.astype(jnp.int32) + has_left.astype(jnp.int32))

    def swap(t, m):
        start = pl.multiple_of((1 - r) * units + t * CHUNK, CHUNK)
        return pltpu.make_async_remote_copy(
            src_ref=(gate, up)[m].at[:, pl.ds(start, CHUNK)],
            dst_ref=w_recv.at[t, m],
            send_sem=x_ss.at[t, m],
            recv_sem=x_rs.at[t, m],
            device_id={"row": 1 - r},
            device_id_type=MESH,
        )

    def own_copy(t, m):
        start = pl.multiple_of(r * units + t * CHUNK, CHUNK)
        slot = lax.rem(t, 2)
        return pltpu.make_async_copy(
            (gate, up)[m].at[:, pl.ds(start, CHUNK)], w_own.at[slot, m], own_sem.at[slot, m]
        )

    def down_copy(t):
        slot = lax.rem(t, 2)
        return pltpu.make_async_copy(
            down.at[pl.ds(pl.multiple_of(t * CHUNK, CHUNK), CHUNK), :], d_own.at[slot], d_sem.at[slot]
        )

    def splat(keep, i, j):
        return jnp.full((BLOCK, BLOCK), keep[i, j].astype(F32), F32).astype(BF16)

    def compute(t):
        slot = lax.rem(t, 2)

        def masked(source, src_row):
            def body(b, carry):
                at = pl.ds(pl.multiple_of(b * BLOCK, BLOCK), BLOCK)
                to = pl.ds(pl.multiple_of(src_row * rows + b * BLOCK, BLOCK), BLOCK)
                for m in range(2):
                    keep = (gate_keep, up_keep)[m]
                    for n in range(CHUNK // BLOCK):
                        s = splat(
                            keep,
                            (z * 2 + src_row) * row_blocks + b,
                            unit_block + t * (CHUNK // BLOCK) + n,
                        )
                        lo = m * CHUNK + n * BLOCK
                        w_mask[to, lo:lo + BLOCK] = (
                            source[m, at, n * BLOCK:(n + 1) * BLOCK] * s
                        )
                return carry

            lax.fori_loop(0, row_blocks, body, 0)

        for m in range(2):
            own_copy(t, m).wait()
        masked(w_own.at[slot], r)
        for m in range(2):
            swap(t, m).wait_recv()
        masked(w_recv.at[t], 1 - r)

        def rows_of(j, carry):
            block = tok[pl.ds(pl.multiple_of(j * shard, shard), shard), :]
            part[slot, j] = jnp.dot(block, w_mask[...], preferred_element_type=F32)
            return carry

        lax.fori_loop(0, Z, rows_of, 0)

    def reduce_copy(t, way, s):
        slot = lax.rem(t, 2)
        return pltpu.make_async_remote_copy(
            src_ref=stage.at[slot, way, s],
            dst_ref=recv.at[t, way, s],
            send_sem=r_ss.at[t, way, s],
            recv_sem=r_rs.at[t, way, s],
            device_id={"depth": z + 1 if way == 0 else z - 1},
            device_id_type=MESH,
        )

    ways = ((0, z, has_right), (1, mirror, has_left))

    def reduce_send(t, s):
        slot = lax.rem(t, 2)
        for way, place, open_way in ways:
            j = Z - 1 - s + place if way == 0 else s - place

            @pl.when(open_way & (place == 0))
            def _():
                stage[slot, way, s] = part[slot, j].astype(BF16)
                reduce_copy(t, way, s).start()

            if s > 0:

                @pl.when(open_way & (place > 0) & (place <= s))
                def _():
                    reduce_copy(t, way, s - 1).wait_recv()
                    stage[slot, way, s] = (
                        part[slot, j] + recv[t, way, s - 1].astype(F32)
                    ).astype(BF16)
                    reduce_copy(t, way, s).start()

    def finish(t):
        slot = lax.rem(t, 2)
        for way, place, _ in ways:

            @pl.when(place > 0)
            def _():
                reduce_copy(t, way, Z - 2).wait_recv()
                part[slot, z] = part[slot, z] + recv[t, way, Z - 2].astype(F32)

        g = part[slot, z, :, :CHUNK]
        u = part[slot, z, :, CHUNK:]
        hid[t, z] = (g / (1.0 + jnp.exp(-g)) * u).astype(BF16)

    def gather_copy(t, way, s):
        j = z - s if way == 0 else z + s
        return pltpu.make_async_remote_copy(
            src_ref=hid.at[t, j],
            dst_ref=hid.at[t, j],
            send_sem=g_ss.at[t, way, s],
            recv_sem=g_rs.at[t, way, s],
            device_id={"depth": z + 1 if way == 0 else z - 1},
            device_id_type=MESH,
        )

    def gather_send(t, s):
        for way, place, open_way in ways:

            @pl.when(open_way & (place >= s))
            def _():
                gather_copy(t, way, s).start()

    def gather_wait(t, s):
        for way, place, _ in ways:

            @pl.when(place >= s + 1)
            def _():
                j = z - 1 - s if way == 0 else z + 1 + s
                pltpu.make_async_remote_copy(
                    src_ref=hid.at[t, j],
                    dst_ref=hid.at[t, j],
                    send_sem=g_ss.at[t, way, s],
                    recv_sem=g_rs.at[t, way, s],
                    device_id={"depth": z - 1 if way == 0 else z + 1},
                    device_id_type=MESH,
                ).wait_recv()

    def add_down(t):
        slot = lax.rem(t, 2)
        down_copy(t).wait()
        wide = 512 if features % 512 == 0 else BLOCK

        def mask_cols(b, carry):
            at = pl.ds(pl.multiple_of(b * BLOCK, BLOCK), BLOCK)
            for n in range(CHUNK // BLOCK):
                s = splat(
                    down_keep,
                    unit_block + t * (CHUNK // BLOCK) + n,
                    z * (features // BLOCK) + b,
                )
                lo = n * BLOCK
                d_mask[lo:lo + BLOCK, at] = d_own[slot, lo:lo + BLOCK, at] * s
            return carry

        lax.fori_loop(0, features // BLOCK, mask_cols, 0)

        def cols_of(n, carry):
            cols = pl.ds(pl.multiple_of(n * wide, wide), wide)

            def rows_of(j, carry):
                at = pl.ds(pl.multiple_of(j * shard, shard), shard)
                mixed[at, cols] += jnp.dot(hid[t, j], d_mask[:, cols], preferred_element_type=F32)
                return carry

            return lax.fori_loop(0, Z, rows_of, carry)

        lax.fori_loop(0, features // wide, cols_of, 0)

    def settle(t):
        for m in range(2):
            swap(t, m).wait_send()
        for way, place, open_way in ways:
            for s in range(Z - 1):

                @pl.when(open_way & (place <= s))
                def _():
                    reduce_copy(t, way, s).wait_send()

                @pl.when(open_way & (place >= s))
                def _():
                    gather_copy(t, way, s).wait_send()

    for t in range(min(AHEAD, K)):
        for m in range(2):
            swap(t, m).start()
    for m in range(2):
        own_copy(0, m).start()

    def clear(j, carry):
        at = pl.ds(pl.multiple_of(j * shard, shard), shard)
        mixed[at, :] = jnp.zeros((shard, features), F32)
        return carry

    lax.fori_loop(0, Z, clear, 0)

    def slot_of(t, carry):
        @pl.when(t < K)
        def _():
            @pl.when(t + 1 < K)
            def _():
                for m in range(2):
                    own_copy(t + 1, m).start()

            down_copy(t).start()
            compute(t)

            @pl.when(t + AHEAD < K)
            def _():
                for m in range(2):
                    swap(t + AHEAD, m).start()

            reduce_send(t, 0)

        @pl.when(t > 0)
        def _():
            finish(t - 1)
            gather_send(t - 1, 0)

        for s in range(1, Z - 1):

            @pl.when(t < K)
            def _():
                reduce_send(t, s)

            @pl.when(t > 0)
            def _():
                gather_wait(t - 1, s - 1)
                gather_send(t - 1, s)

        @pl.when(t > 0)
        def _():
            gather_wait(t - 1, Z - 2)
            add_down(t - 1)
            settle(t - 1)

        return carry

    lax.fori_loop(0, K + 1, slot_of, 0)


def layer_call(tok, gate, up, down, gate_keep, up_keep, down_keep):
    Z = lax.axis_size("depth")
    T, rows = tok.shape[0], gate.shape[0]
    units, features = down.shape
    K, shard = units // CHUNK, T // Z
    dma = pltpu.SemaphoreType.DMA
    vmem = pl.BlockSpec(memory_space=pltpu.VMEM)
    smem = pl.BlockSpec(memory_space=pltpu.SMEM)
    any_space = pl.BlockSpec(memory_space=pl.ANY)
    return pl.pallas_call(
        functools.partial(layer_kernel, Z),
        out_shape=jax.ShapeDtypeStruct((T, features), F32),
        in_specs=[vmem, any_space, any_space, any_space, smem, smem, smem],
        out_specs=vmem,
        scratch_shapes=[
            pltpu.VMEM((K, 2, rows, CHUNK), BF16),
            pltpu.VMEM((2, 2, rows, CHUNK), BF16),
            pltpu.VMEM((2 * rows, 2 * CHUNK), BF16),
            pltpu.VMEM((2, CHUNK, features), BF16),
            pltpu.VMEM((CHUNK, features), BF16),
            pltpu.VMEM((2, Z, shard, 2 * CHUNK), F32),
            pltpu.VMEM((2, 2, Z - 1, shard, 2 * CHUNK), BF16),
            pltpu.VMEM((K, 2, Z - 1, shard, 2 * CHUNK), BF16),
            pltpu.VMEM((K, Z, shard, CHUNK), BF16),
            dma((K, 2)), dma((K, 2)), dma((2, 2)), dma((2,)),
            dma((K, 2, Z - 1)), dma((K, 2, Z - 1)), dma((K, 2, Z - 1)), dma((K, 2, Z - 1)),
        ],
        compiler_params=pltpu.CompilerParams(
            collective_id=0, has_side_effects=True, vmem_limit_bytes=60 * 1024 * 1024
        ),
        cost_estimate=pl.CostEstimate(
            flops=6 * T * units * features, bytes_accessed=6 * units * features, transcendentals=0
        ),
    )(tok, gate, up, down, gate_keep, up_keep, down_keep)


def keep_table(keep, row_start, col_start, row_count, col_count):
    row_ids = (row_start + jnp.arange(row_count, dtype=jnp.int32)) // BLOCK
    col_ids = (col_start + jnp.arange(col_count, dtype=jnp.int32)) // BLOCK
    pick_rows = (row_ids[:, None] == jnp.arange(keep.shape[0], dtype=jnp.int32)[None, :]).astype(BF16)
    pick_cols = (jnp.arange(keep.shape[1], dtype=jnp.int32)[:, None] == col_ids[None, :]).astype(BF16)
    inner = jnp.dot(keep.astype(BF16), pick_cols, preferred_element_type=F32).astype(BF16)
    return jnp.dot(pick_rows, inner, preferred_element_type=F32).astype(BF16)


def plain_layer(token_block, gate_weight, up_weight, down_weight, gate_keep, up_keep, down_keep):
    row_total = lax.axis_size("row")
    units, features = down_weight.shape
    feature_start = lax.axis_index("depth") * features
    unit_start = (lax.axis_index("col") * row_total + lax.axis_index("row")) * units

    def total(weight, keep):
        whole = lax.all_to_all(weight, "row", split_axis=1, concat_axis=0, tiled=True)
        masked = whole * keep_table(keep, feature_start, unit_start, features, units)
        part = jnp.dot(token_block, masked, preferred_element_type=F32)
        return lax.psum_scatter(part, "depth", scatter_dimension=0, tiled=True)

    gate = total(gate_weight, gate_keep)
    hidden = (jax.nn.silu(gate) * total(up_weight, up_keep)).astype(BF16)
    hidden = lax.all_gather(hidden, "depth", axis=0, tiled=True)
    down_masked = down_weight * keep_table(down_keep, unit_start, feature_start, units, features)
    return jnp.dot(hidden, down_masked, preferred_element_type=F32)


def on_device(tokens, gate_weight, up_weight, down_weight, *keeps):
    Z = lax.axis_size("depth")
    units, features = down_weight.shape
    token_block = lax.all_gather(tokens, ("row", "col"), axis=0, tiled=True)
    fits = (
        lax.axis_size("row") == 2
        and Z > 1
        and units % CHUNK == 0
        and gate_weight.shape[0] % BLOCK == 0
        and features % BLOCK == 0
        and token_block.shape[0] % (16 * Z) == 0
        and token_block.shape[0] <= 1024
    )
    layer = layer_call if fits else plain_layer
    mixed = layer(token_block, gate_weight, up_weight, down_weight, *keeps)
    mixed = lax.psum_scatter(mixed, ("row", "col"), scatter_dimension=0, tiled=True)
    return mixed.astype(BF16)


def solution(mesh):
    placed = (
        P(("row", "col"), "depth"),
        P(("depth", "row"), "col"),
        P(("depth", "row"), "col"),
        P(("col", "row"), "depth"),
        P(),
        P(),
        P(),
    )
    return jax.shard_map(
        on_device, mesh=mesh, in_specs=placed, out_specs=P(("row", "col"), "depth"), check_vma=False
    )
```

time: 1130 us -> 367 us (0.32)
  waiting for transfers between devices: 1030 us -> 113 us
  Pallas kernels: 0 us -> 236 us
  matrix products: 65.3 us -> 0 us
  other arithmetic: 17.3 us -> 2.08 us
    psum x1 -> x0, waiting for transfers between devices: 496 us -> none  [on_device(): total = lax.psum(both, 'depth')]
    all_gather x4 -> x1, waiting for transfers between devices: 492 us -> 39.9 us  [on_device(): token_block = lax.all_gather(tokens, ('row', 'col'), axis=0, tiled=True)]
    pallas_call x0 -> x1, Pallas kernels: none -> 236 us  [layer_call(): pl.pallas_call(functools.partial(layer_kernel, Z), out_shape=jax.ShapeDty...]
    dot_general x6 -> x0, matrix products: 65.3 us -> none  [the longest x2 27.6 us: add_panel(): return jnp.dot(token_block, piece, preferred_element_type=jnp.float32)]
    reduce_scatter x1, waiting for transfers between devices: 43.5 us -> 72.6 us  [on_device(): lax.psum_scatter(mixed, ('row', 'col'), scatter_dimension=0, tiled=True)]
    another operation x1 -> x0, other arithmetic: 15.1 us -> none  [on_device(): both = jnp.stack((gate, up), 0)]
  transfers between devices with their start and end apart: 6 -> 2, of which waited for: 6 -> 2; matrix products, arithmetic and copies ran while one was open for 6% -> 0% of each run, Pallas kernels for 0% -> 0%
where the time goes in v1:
time: 367 us
  Pallas kernels  236 us (64%)
  waiting for transfers between devices  113 us (31%)
  between operations  13.4 us (4%)
    pallas_call x1, Pallas kernels, layer_call(): pl.pallas_call(functools.partial(layer_kernel, Z), out_shape=jax.ShapeDty...  236 us
    reduce_scatter x1, waiting for transfers between devices, on_device(): lax.psum_scatter(mixed, ('row', 'col'), scatter_dimension=0, tiled=True)  72.6 us
    all_gather x1, waiting for transfers between devices, on_device(): token_block = lax.all_gather(tokens, ('row', 'col'), axis=0, tiled=True)  39.9 us
  transfers between devices with their start and end apart: 2, of which 2 were waited for; matrix products, arithmetic and copies ran while one was open for 0% of the time, Pallas kernels for 0%

profile of v1, /device:TPU:0, one launch (start us, length us, event | category | flops | bytes accessed | tf_op | source)
XLA Modules:
  0.0 366.6 jit_solution(2189753786482368543)
XLA Ops:
  6.5 0.0 all-gather.2.cloned.1.call-start
  6.5 0.7 all-gather.2.cloned.1.call-update
  7.3 0.0 reduce-scatter.2.cloned.1.call-start
  7.3 1.5 copy.8.down_keep
  8.8 39.9 %all-gather.2.cloned.1.call-done.tok = bf16[1024,2048]{1,0:T(8,128)(2,1)} async-done(((bf16[128,2048]{1,0:T(8,128)(2,1)}), bf16[1024,2048]{1,0:T(8,128)(2,1)}) %all-gather.2.cloned.1.call-update) | async-done | bytes 4194320 | tf_op jit(solution)/shard_map/all_gather | solution.py:360
  48.7 236.4 %shard_map.73 = f32[1024,2048]{1,0:T(8,128)} custom-call(bf16[1024,2048]{1,0:T(8,128)(2,1)} %all-gather.2.cloned.1.call-done.tok, bf16[1024,3584]{1,0:T(8,128)(2,1)} %gate.1, bf16[1024,3584]{1,0:T(8,128)(2,1)} %up.1, bf16[1792,2048]{1,0:T(8,128)(2,1)} %down.1, s32[64,112]{1,0:T(8,128)} %gate_keep.1, s32[64,112]{1,0:T(8,128)} %up_keep.1, s32[112,64]{1,0:T(8,128)} %copy.8.down_keep), custom_call_target="tpu_custom_call" | custom-call | flops 22548578304 | bytes 22020096 | tf_op jit(solution)/shard_map/pallas_call | solution.py:302
  285.1 0.0 reduce-scatter.2.cloned.1.call-update
  285.1 72.6 %reduce-scatter.2.cloned.1.call-done = f32[128,2048]{1,0:T(8,128)} async-done(((f32[1024,2048]{1,0:T(8,128)}), f32[128,2048]{1,0:T(8,128)}) %reduce-scatter.2.cloned.1.call-update) | async-done | bytes 1048592 | tf_op jit(solution)/shard_map/reduce_scatter | solution.py:372
  357.7 2.1 convert_element_type.3
Async XLA Ops:
  6.5 42.2 %all-gather.2.cloned.1.call-start = ((), (), s32[]{:S(2)}) async-start(), calls=%async_computation.1 | async-start | bytes 4718592 | tf_op jit(solution)/shard_map/all_gather | solution.py:360
  7.3 350.5 %reduce-scatter.2.cloned.1.call-start = ((), (), s32[]{:S(2)}) async-start(), calls=%async_computation.2 | async-start | bytes 9437184 | tf_op jit(solution)/shard_map/reduce_scatter | solution.py:372
Sparse Core Ops, SparseCore 0:
  9.2 39.4 all-gather.1
  285.2 72.4 reduce-scatter.1

commit v2 on v1

--- a/solution.py
+++ b/solution.py
@@ -16,9 +16,11 @@
 
 
 def layer_kernel(
-    Z, tok, gate, up, down, gate_keep, up_keep, down_keep, mixed,
-    w_recv, w_own, w_mask, d_own, d_mask, part, stage, recv, hid,
-    x_ss, x_rs, own_sem, d_sem, r_ss, r_rs, g_ss, g_rs,
+    Z, tokens, gate, up, down, gate_keep, up_keep, down_keep, out,
+    tok, mixed, w_recv, w_own, w_mask, d_own, d_mask, part, stage, recv, hid,
+    core_recv, y_stage, y_recv, row_stage, row_recv,
+    x_ss, x_rs, own_sem, d_sem, r_ss, r_rs, g_ss, g_rs, t_ss, t_rs, t_own,
+    c_ss, c_rs, y_ss, y_rs, o_ss, o_rs,
 ):
     z, r, c = lax.axis_index("depth"), lax.axis_index("row"), lax.axis_index("col")
     K = w_recv.shape[0]
@@ -30,9 +32,16 @@
     unit_block = (c * 2 + r) * (units // BLOCK)
     has_right, has_left = z < Z - 1, z > 0
     mirror = Z - 1 - z
+    held = tokens.shape[0]
+    wide = 512 if features % 512 == 0 else BLOCK
+    pieces = features // wide
+    core_mate = c + 1 - 2 * lax.rem(c, 2)
+    y_mate = lax.rem(c + 2, 4)
+    mates = ({"row": 1 - r}, {"col": y_mate}, {"col": core_mate})
 
     barrier = pltpu.get_barrier_semaphore()
-    pl.semaphore_signal(barrier, inc=1, device_id={"row": 1 - r}, device_id_type=MESH)
+    for mate in mates:
+        pl.semaphore_signal(barrier, inc=1, device_id=mate, device_id_type=MESH)
 
     @pl.when(has_right)
     def _():
@@ -42,7 +51,46 @@
     def _():
         pl.semaphore_signal(barrier, inc=1, device_id={"depth": z - 1}, device_id_type=MESH)
 
-    pl.semaphore_wait(barrier, 1 + has_right.astype(jnp.int32) + has_left.astype(jnp.int32))
+    pl.semaphore_wait(barrier, 3 + has_right.astype(jnp.int32) + has_left.astype(jnp.int32))
+
+    def rows_at(row, col):
+        return pl.ds(pl.multiple_of((row * 4 + col) * held, held), held)
+
+    token_moves = (
+        (r, c, 1 - r, c, 0),
+        (r, c, r, y_mate, 1),
+        (1 - r, c, 1 - r, y_mate, 1),
+        (r, c, r, core_mate, 2),
+        (1 - r, c, 1 - r, core_mate, 2),
+        (r, y_mate, r, lax.rem(core_mate + 2, 4), 2),
+        (1 - r, y_mate, 1 - r, lax.rem(core_mate + 2, 4), 2),
+    )
+
+    def token_copy(i, arriving=False):
+        row, col, back_row, back_col, mate = token_moves[i]
+        at = rows_at(back_row, back_col) if arriving else rows_at(row, col)
+        return pltpu.make_async_remote_copy(
+            src_ref=tokens if i in (0, 1, 3) else tok.at[at],
+            dst_ref=tok.at[at],
+            send_sem=t_ss.at[i],
+            recv_sem=t_rs.at[i],
+            device_id=mates[mate],
+            device_id_type=MESH,
+        )
+
+    def tokens_in():
+        token_copy(0, True).wait_recv()
+        token_copy(2).start()
+        token_copy(4).start()
+        token_copy(1, True).wait_recv()
+        token_copy(5).start()
+        token_copy(2, True).wait_recv()
+        token_copy(6).start()
+        for i in (3, 4, 5, 6):
+            token_copy(i, True).wait_recv()
+        for i in range(7):
+            token_copy(i).wait_send()
+        pltpu.make_async_copy(tokens, tok.at[rows_at(r, c)], t_own).wait()
 
     def swap(t, m):
         start = pl.multiple_of((1 - r) * units + t * CHUNK, CHUNK)
@@ -189,8 +237,8 @@
 
     def add_down(t):
         slot = lax.rem(t, 2)
+        gather_wait(t, Z - 2)
         down_copy(t).wait()
-        wide = 512 if features % 512 == 0 else BLOCK
 
         def mask_cols(b, carry):
             at = pl.ds(pl.multiple_of(b * BLOCK, BLOCK), BLOCK)
@@ -214,11 +262,18 @@
                 mixed[at, cols] += jnp.dot(hid[t, j], d_mask[:, cols], preferred_element_type=F32)
                 return carry
 
-            return lax.fori_loop(0, Z, rows_of, carry)
-
-        lax.fori_loop(0, features // wide, cols_of, 0)
-
-    def settle(t):
+            lax.fori_loop(0, Z, rows_of, 0)
+
+            @pl.when(t == K - 1)
+            def _():
+                for i in range(4):
+                    core_copy(n, i).start()
+
+            return carry
+
+        lax.fori_loop(0, pieces, cols_of, 0)
+
+    def settle_reduce(t):
         for m in range(2):
             swap(t, m).wait_send()
         for way, place, open_way in ways:
@@ -228,10 +283,85 @@
                 def _():
                     reduce_copy(t, way, s).wait_send()
 
+    def settle_gather(t):
+        for way, place, open_way in ways:
+            for s in range(Z - 1):
+
                 @pl.when(open_way & (place >= s))
                 def _():
                     gather_copy(t, way, s).wait_send()
 
+    core, y = lax.rem(c, 2), c // 2
+
+    def cols_at(n):
+        return pl.ds(pl.multiple_of(n * wide, wide), wide)
+
+    def core_copy(n, i):
+        return pltpu.make_async_remote_copy(
+            src_ref=mixed.at[rows_at(i // 2, (i % 2) * 2 + 1 - core), cols_at(n)],
+            dst_ref=core_recv.at[n, i],
+            send_sem=c_ss.at[n, i],
+            recv_sem=c_rs.at[n, i],
+            device_id=mates[2],
+            device_id_type=MESH,
+        )
+
+    def y_copy(n):
+        return pltpu.make_async_remote_copy(
+            src_ref=y_stage.at[n],
+            dst_ref=y_recv.at[n],
+            send_sem=y_ss.at[n],
+            recv_sem=y_rs.at[n],
+            device_id=mates[1],
+            device_id_type=MESH,
+        )
+
+    def row_copy(n):
+        return pltpu.make_async_remote_copy(
+            src_ref=row_stage.at[n],
+            dst_ref=row_recv.at[n],
+            send_sem=o_ss.at[n],
+            recv_sem=o_rs.at[n],
+            device_id=mates[0],
+            device_id_type=MESH,
+        )
+
+    def after_core(n, carry):
+        for i in range(4):
+            core_copy(n, i).wait_recv()
+        for row in range(2):
+            y_stage[n, row] = (
+                mixed[rows_at(row, (1 - y) * 2 + core), cols_at(n)] + core_recv[n, row * 2 + 1 - y]
+            ).astype(BF16)
+        y_copy(n).start()
+        return carry
+
+    def after_y(n, carry):
+        y_copy(n).wait_recv()
+        at = rows_at(1 - r, c)
+        row_stage[n] = (
+            mixed[at, cols_at(n)] + core_recv[n, (1 - r) * 2 + y] + y_recv[n, 1 - r].astype(F32)
+        ).astype(BF16)
+        row_copy(n).start()
+        return carry
+
+    def after_row(n, carry):
+        row_copy(n).wait_recv()
+        out[:, cols_at(n)] = (
+            mixed[rows_at(r, c), cols_at(n)]
+            + core_recv[n, r * 2 + y]
+            + y_recv[n, r].astype(F32)
+            + row_recv[n].astype(F32)
+        ).astype(BF16)
+        for i in range(4):
+            core_copy(n, i).wait_send()
+        y_copy(n).wait_send()
+        row_copy(n).wait_send()
+        return carry
+
+    for i in (0, 1, 3):
+        token_copy(i).start()
+    pltpu.make_async_copy(tokens, tok.at[rows_at(r, c)], t_own).start()
     for t in range(min(AHEAD, K)):
         for m in range(2):
             swap(t, m).start()
@@ -253,7 +383,6 @@
                 for m in range(2):
                     own_copy(t + 1, m).start()
 
-            down_copy(t).start()
             compute(t)
 
             @pl.when(t + AHEAD < K)
@@ -263,48 +392,66 @@
 
             reduce_send(t, 0)
 
-        @pl.when(t > 0)
+        before = (t > 0) & (t <= K)
+
+        @pl.when(before)
         def _():
+            down_copy(t - 1).start()
             finish(t - 1)
             gather_send(t - 1, 0)
 
+        @pl.when(t > 1)
+        def _():
+            add_down(t - 2)
+
         for s in range(1, Z - 1):
 
             @pl.when(t < K)
             def _():
                 reduce_send(t, s)
 
-            @pl.when(t > 0)
+            @pl.when(before)
             def _():
                 gather_wait(t - 1, s - 1)
                 gather_send(t - 1, s)
 
-        @pl.when(t > 0)
+        @pl.when(before)
         def _():
-            gather_wait(t - 1, Z - 2)
-            add_down(t - 1)
-            settle(t - 1)
+            settle_reduce(t - 1)
+
+        @pl.when(t > 1)
+        def _():
+            settle_gather(t - 2)
 
         return carry
 
-    lax.fori_loop(0, K + 1, slot_of, 0)
-
-
-def layer_call(tok, gate, up, down, gate_keep, up_keep, down_keep):
+    tokens_in()
+    lax.fori_loop(0, K + 2, slot_of, 0)
+    lax.fori_loop(0, pieces, after_core, 0)
+    lax.fori_loop(0, pieces, after_y, 0)
+    lax.fori_loop(0, pieces, after_row, 0)
+
+
+def layer_call(tokens, gate, up, down, gate_keep, up_keep, down_keep):
     Z = lax.axis_size("depth")
-    T, rows = tok.shape[0], gate.shape[0]
+    held, rows = tokens.shape[0], gate.shape[0]
+    T = held * 8
     units, features = down.shape
     K, shard = units // CHUNK, T // Z
+    wide = 512 if features % 512 == 0 else BLOCK
+    pieces = features // wide
     dma = pltpu.SemaphoreType.DMA
     vmem = pl.BlockSpec(memory_space=pltpu.VMEM)
     smem = pl.BlockSpec(memory_space=pltpu.SMEM)
     any_space = pl.BlockSpec(memory_space=pl.ANY)
     return pl.pallas_call(
         functools.partial(layer_kernel, Z),
-        out_shape=jax.ShapeDtypeStruct((T, features), F32),
+        out_shape=jax.ShapeDtypeStruct((held, features), BF16),
         in_specs=[vmem, any_space, any_space, any_space, smem, smem, smem],
         out_specs=vmem,
         scratch_shapes=[
+            pltpu.VMEM((T, features), BF16),
+            pltpu.VMEM((T, features), F32),
             pltpu.VMEM((K, 2, rows, CHUNK), BF16),
             pltpu.VMEM((2, 2, rows, CHUNK), BF16),
             pltpu.VMEM((2 * rows, 2 * CHUNK), BF16),
@@ -314,16 +461,24 @@
             pltpu.VMEM((2, 2, Z - 1, shard, 2 * CHUNK), BF16),
             pltpu.VMEM((K, 2, Z - 1, shard, 2 * CHUNK), BF16),
             pltpu.VMEM((K, Z, shard, CHUNK), BF16),
+            pltpu.VMEM((pieces, 4, held, wide), F32),
+            pltpu.VMEM((pieces, 2, held, wide), BF16),
+            pltpu.VMEM((pieces, 2, held, wide), BF16),
+            pltpu.VMEM((pieces, held, wide), BF16),
+            pltpu.VMEM((pieces, held, wide), BF16),
             dma((K, 2)), dma((K, 2)), dma((2, 2)), dma((2,)),
             dma((K, 2, Z - 1)), dma((K, 2, Z - 1)), dma((K, 2, Z - 1)), dma((K, 2, Z - 1)),
+            dma((7,)), dma((7,)), dma,
+            dma((pieces, 4)), dma((pieces, 4)), dma((pieces,)), dma((pieces,)),
+            dma((pieces,)), dma((pieces,)),
         ],
         compiler_params=pltpu.CompilerParams(
-            collective_id=0, has_side_effects=True, vmem_limit_bytes=60 * 1024 * 1024
+            collective_id=0, has_side_effects=True, vmem_limit_bytes=62 * 1024 * 1024
         ),
         cost_estimate=pl.CostEstimate(
             flops=6 * T * units * features, bytes_accessed=6 * units * features, transcendentals=0
         ),
-    )(tok, gate, up, down, gate_keep, up_keep, down_keep)
+    )(tokens, gate, up, down, gate_keep, up_keep, down_keep)
 
 
 def keep_table(keep, row_start, col_start, row_count, col_count):
@@ -357,18 +512,21 @@
 def on_device(tokens, gate_weight, up_weight, down_weight, *keeps):
     Z = lax.axis_size("depth")
     units, features = down_weight.shape
-    token_block = lax.all_gather(tokens, ("row", "col"), axis=0, tiled=True)
     fits = (
         lax.axis_size("row") == 2
+        and lax.axis_size("col") == 4
         and Z > 1
         and units % CHUNK == 0
         and gate_weight.shape[0] % BLOCK == 0
         and features % BLOCK == 0
-        and token_block.shape[0] % (16 * Z) == 0
-        and token_block.shape[0] <= 1024
+        and tokens.shape[0] * 8 % (16 * Z) == 0
+        and tokens.shape[0] % 16 == 0
+        and tokens.shape[0] <= 128
     )
-    layer = layer_call if fits else plain_layer
-    mixed = layer(token_block, gate_weight, up_weight, down_weight, *keeps)
+    if fits:
+        return layer_call(tokens, gate_weight, up_weight, down_weight, *keeps)
+    token_block = lax.all_gather(tokens, ("row", "col"), axis=0, tiled=True)
+    mixed = plain_layer(token_block, gate_weight, up_weight, down_weight, *keeps)
     mixed = lax.psum_scatter(mixed, ("row", "col"), scatter_dimension=0, tiled=True)
     return mixed.astype(BF16)
 

time: 367 us -> 256 us (0.70)
  waiting for transfers between devices: 113 us -> 0 us
  Pallas kernels: 236 us -> 253 us
  between operations: 13.4 us -> 0.01 us
    reduce_scatter x1 -> x0, waiting for transfers between devices: 72.6 us -> none  [on_device(): lax.psum_scatter(mixed, ('row', 'col'), scatter_dimension=0, tiled=True)]
    all_gather x1 -> x0, waiting for transfers between devices: 39.9 us -> none  [on_device(): token_block = lax.all_gather(tokens, ('row', 'col'), axis=0, tiled=True)]
    pallas_call x1, Pallas kernels: 236 us -> 253 us  [layer_call(): pl.pallas_call(functools.partial(layer_kernel, Z), out_shape=jax.ShapeDty...]
  transfers between devices with their start and end apart: 2 -> 0, of which waited for: 2 -> 0; matrix products, arithmetic and copies ran while one was open for 0% -> 0% of each run, Pallas kernels for 0% -> 0%
where the time goes in v2:
time: 256 us
  Pallas kernels  253 us (99%)
  local copies, waits for them, and re-layouts  3.36 us (1%)
    pallas_call x1, Pallas kernels, layer_call(): pl.pallas_call(functools.partial(layer_kernel, Z), out_shape=jax.ShapeDty...  253 us

profile of v2, /device:TPU:0, one launch (start us, length us, event | category | flops | bytes accessed | tf_op | source)
XLA Modules:
  0.0 256.0 jit_solution(17176631426571891780)
XLA Ops:
  0.0 1.5 copy.8.down_keep
  1.5 252.6 %shard_map.73 = bf16[128,2048]{1,0:T(8,128)(2,1)} custom-call(bf16[128,2048]{1,0:T(8,128)(2,1)} %tokens.1, bf16[1024,3584]{1,0:T(8,128)(2,1)} %gate.1, bf16[1024,3584]{1,0:T(8,128)(2,1)} %up.1, bf16[1792,2048]{1,0:T(8,128)(2,1)} %down.1, s32[64,112]{1,0:T(8,128)} %gate_keep.1, s32[64,112]{1,0:T(8,128)} %up_keep.1, s32[112,64]{1,0:T(8,128)} %copy.8.down_keep), custom_call_target="tpu_custom_call" | custom-call | flops 22548578304 | bytes 22020096 | tf_op jit(solution)/shard_map/pallas_call | solution.py:447
  254.1 1.9 copy.10

commit v3 on v2

--- a/solution.py
+++ b/solution.py
@@ -8,7 +8,7 @@
 from jax.sharding import PartitionSpec as P
 
 BLOCK = 128
-CHUNK = 256
+CHUNK = 128
 AHEAD = 3
 MESH = pl.DeviceIdType.MESH
 BF16 = jnp.bfloat16
@@ -151,7 +151,7 @@
 
         def rows_of(j, carry):
             block = tok[pl.ds(pl.multiple_of(j * shard, shard), shard), :]
-            part[slot, j] = jnp.dot(block, w_mask[...], preferred_element_type=F32)
+            part[lax.rem(t, Z), j] = jnp.dot(block, w_mask[...], preferred_element_type=F32)
             return carry
 
         lax.fori_loop(0, Z, rows_of, 0)
@@ -170,13 +170,13 @@
     ways = ((0, z, has_right), (1, mirror, has_left))
 
     def reduce_send(t, s):
-        slot = lax.rem(t, 2)
+        slot, live = lax.rem(t, 2), lax.rem(t, Z)
         for way, place, open_way in ways:
             j = Z - 1 - s + place if way == 0 else s - place
 
             @pl.when(open_way & (place == 0))
             def _():
-                stage[slot, way, s] = part[slot, j].astype(BF16)
+                stage[slot, way, s] = part[live, j].astype(BF16)
                 reduce_copy(t, way, s).start()
 
             if s > 0:
@@ -185,21 +185,21 @@
                 def _():
                     reduce_copy(t, way, s - 1).wait_recv()
                     stage[slot, way, s] = (
-                        part[slot, j] + recv[t, way, s - 1].astype(F32)
+                        part[live, j] + recv[t, way, s - 1].astype(F32)
                     ).astype(BF16)
                     reduce_copy(t, way, s).start()
 
     def finish(t):
-        slot = lax.rem(t, 2)
+        live = lax.rem(t, Z)
         for way, place, _ in ways:
 
             @pl.when(place > 0)
             def _():
                 reduce_copy(t, way, Z - 2).wait_recv()
-                part[slot, z] = part[slot, z] + recv[t, way, Z - 2].astype(F32)
-
-        g = part[slot, z, :, :CHUNK]
-        u = part[slot, z, :, CHUNK:]
+                part[live, z] = part[live, z] + recv[t, way, Z - 2].astype(F32)
+
+        g = part[live, z, :, :CHUNK]
+        u = part[live, z, :, CHUNK:]
         hid[t, z] = (g / (1.0 + jnp.exp(-g)) * u).astype(BF16)
 
     def gather_copy(t, way, s):
@@ -273,28 +273,29 @@
 
         lax.fori_loop(0, pieces, cols_of, 0)
 
-    def settle_reduce(t):
+    def settle_reduce(t, s):
+        for way, place, open_way in ways:
+
+            @pl.when(open_way & (place <= s))
+            def _():
+                reduce_copy(t, way, s).wait_send()
+
+    def settle(t, carry):
         for m in range(2):
             swap(t, m).wait_send()
         for way, place, open_way in ways:
             for s in range(Z - 1):
 
-                @pl.when(open_way & (place <= s))
-                def _():
-                    reduce_copy(t, way, s).wait_send()
-
-    def settle_gather(t):
-        for way, place, open_way in ways:
-            for s in range(Z - 1):
-
                 @pl.when(open_way & (place >= s))
                 def _():
                     gather_copy(t, way, s).wait_send()
 
+        return carry
+
     core, y = lax.rem(c, 2), c // 2
 
     def cols_at(n):
-        return pl.ds(pl.multiple_of(n * wide, wide), wide)
+        return pl.ds(n * wide if isinstance(n, int) else pl.multiple_of(n * wide, wide), wide)
 
     def core_copy(n, i):
         return pltpu.make_async_remote_copy(
@@ -306,58 +307,54 @@
             device_id_type=MESH,
         )
 
-    def y_copy(n):
+    def first_copy(n):
         return pltpu.make_async_remote_copy(
             src_ref=y_stage.at[n],
             dst_ref=y_recv.at[n],
             send_sem=y_ss.at[n],
             recv_sem=y_rs.at[n],
-            device_id=mates[1],
-            device_id_type=MESH,
-        )
-
-    def row_copy(n):
+            device_id=mates[1 - n % 2],
+            device_id_type=MESH,
+        )
+
+    def second_copy(n):
         return pltpu.make_async_remote_copy(
             src_ref=row_stage.at[n],
             dst_ref=row_recv.at[n],
             send_sem=o_ss.at[n],
             recv_sem=o_rs.at[n],
-            device_id=mates[0],
-            device_id_type=MESH,
-        )
-
-    def after_core(n, carry):
+            device_id=mates[n % 2],
+            device_id_type=MESH,
+        )
+
+    def chip_sum(n, row, place):
+        return mixed[rows_at(row, place * 2 + core), cols_at(n)] + core_recv[n, row * 2 + place]
+
+    def after_core(n):
         for i in range(4):
             core_copy(n, i).wait_recv()
-        for row in range(2):
-            y_stage[n, row] = (
-                mixed[rows_at(row, (1 - y) * 2 + core), cols_at(n)] + core_recv[n, row * 2 + 1 - y]
-            ).astype(BF16)
-        y_copy(n).start()
-        return carry
-
-    def after_y(n, carry):
-        y_copy(n).wait_recv()
-        at = rows_at(1 - r, c)
-        row_stage[n] = (
-            mixed[at, cols_at(n)] + core_recv[n, (1 - r) * 2 + y] + y_recv[n, 1 - r].astype(F32)
-        ).astype(BF16)
-        row_copy(n).start()
-        return carry
-
-    def after_row(n, carry):
-        row_copy(n).wait_recv()
-        out[:, cols_at(n)] = (
-            mixed[rows_at(r, c), cols_at(n)]
-            + core_recv[n, r * 2 + y]
-            + y_recv[n, r].astype(F32)
-            + row_recv[n].astype(F32)
-        ).astype(BF16)
+        for i in range(2):
+            total = chip_sum(n, i, 1 - y) if n % 2 == 0 else chip_sum(n, 1 - r, i)
+            y_stage[n, i] = total.astype(BF16)
+        first_copy(n).start()
+
+    def after_first(n):
+        first_copy(n).wait_recv()
+        if n % 2 == 0:
+            total = chip_sum(n, 1 - r, y) + y_recv[n, 1 - r].astype(F32)
+        else:
+            total = chip_sum(n, r, 1 - y) + y_recv[n, 1 - y].astype(F32)
+        row_stage[n] = total.astype(BF16)
+        second_copy(n).start()
+
+    def after_second(n):
+        second_copy(n).wait_recv()
+        total = chip_sum(n, r, y) + y_recv[n, r if n % 2 == 0 else y].astype(F32)
+        out[:, cols_at(n)] = (total + row_recv[n].astype(F32)).astype(BF16)
         for i in range(4):
             core_copy(n, i).wait_send()
-        y_copy(n).wait_send()
-        row_copy(n).wait_send()
-        return carry
+        first_copy(n).wait_send()
+        second_copy(n).wait_send()
 
     for i in (0, 1, 3):
         token_copy(i).start()
@@ -392,44 +389,42 @@
 
             reduce_send(t, 0)
 
-        before = (t > 0) & (t <= K)
-
-        @pl.when(before)
-        def _():
-            down_copy(t - 1).start()
-            finish(t - 1)
-            gather_send(t - 1, 0)
-
-        @pl.when(t > 1)
-        def _():
-            add_down(t - 2)
-
+        def at_chunk(lag, work):
+            @pl.when((t >= lag) & (t < K + lag))
+            def _():
+                work(t - lag)
+
+        last = 2 * Z - 2
+        at_chunk(last - 1, lambda k: down_copy(k).start())
         for s in range(1, Z - 1):
-
-            @pl.when(t < K)
-            def _():
-                reduce_send(t, s)
-
-            @pl.when(before)
-            def _():
-                gather_wait(t - 1, s - 1)
-                gather_send(t - 1, s)
-
-        @pl.when(before)
-        def _():
-            settle_reduce(t - 1)
-
-        @pl.when(t > 1)
-        def _():
-            settle_gather(t - 2)
-
+            at_chunk(s, functools.partial(reduce_send, s=s))
+
+        def finish_and_send(k):
+            finish(k)
+            gather_send(k, 0)
+
+        at_chunk(Z - 1, finish_and_send)
+
+        def pass_on(k, s):
+            gather_wait(k, s - 1)
+            gather_send(k, s)
+
+        for s in range(1, Z - 1):
+            at_chunk(Z - 1 + s, functools.partial(pass_on, s=s))
+        at_chunk(last, add_down)
+        for s in range(Z - 1):
+            at_chunk(s + 1, functools.partial(settle_reduce, s=s))
         return carry
 
     tokens_in()
-    lax.fori_loop(0, K + 2, slot_of, 0)
-    lax.fori_loop(0, pieces, after_core, 0)
-    lax.fori_loop(0, pieces, after_y, 0)
-    lax.fori_loop(0, pieces, after_row, 0)
+    lax.fori_loop(0, K + 2 * Z - 2, slot_of, 0)
+    for n in range(pieces):
+        after_core(n)
+    for n in range(pieces):
+        after_first(n)
+    for n in range(pieces):
+        after_second(n)
+    lax.fori_loop(0, K, settle, 0)
 
 
 def layer_call(tokens, gate, up, down, gate_keep, up_keep, down_keep):
@@ -457,7 +452,7 @@
             pltpu.VMEM((2 * rows, 2 * CHUNK), BF16),
             pltpu.VMEM((2, CHUNK, features), BF16),
             pltpu.VMEM((CHUNK, features), BF16),
-            pltpu.VMEM((2, Z, shard, 2 * CHUNK), F32),
+            pltpu.VMEM((Z, Z, shard, 2 * CHUNK), F32),
             pltpu.VMEM((2, 2, Z - 1, shard, 2 * CHUNK), BF16),
             pltpu.VMEM((K, 2, Z - 1, shard, 2 * CHUNK), BF16),
             pltpu.VMEM((K, Z, shard, CHUNK), BF16),

time: 256 us -> 249 us (0.973)
  Pallas kernels: 253 us -> 245 us
    pallas_call x1, Pallas kernels: 253 us -> 245 us  [layer_call(): pl.pallas_call(functools.partial(layer_kernel, Z), out_shape=jax.ShapeDty...]
where the time goes in v3:
time: 249 us; the launch traced here: 248 us
  Pallas kernels  245 us (98%)
  local copies, waits for them, and re-layouts  3.36 us (1%)
    pallas_call x1, Pallas kernels, layer_call(): pl.pallas_call(functools.partial(layer_kernel, Z), out_shape=jax.ShapeDty...  245 us

profile of v3, /device:TPU:0, one launch (start us, length us, event | category | flops | bytes accessed | tf_op | source)
XLA Modules:
  0.0 248.4 jit_solution(7967656177880917013)
XLA Ops:
  0.0 1.5 copy.8.down_keep
  1.5 245.0 %shard_map.73 = bf16[128,2048]{1,0:T(8,128)(2,1)} custom-call(bf16[128,2048]{1,0:T(8,128)(2,1)} %tokens.1, bf16[1024,3584]{1,0:T(8,128)(2,1)} %gate.1, bf16[1024,3584]{1,0:T(8,128)(2,1)} %up.1, bf16[1792,2048]{1,0:T(8,128)(2,1)} %down.1, s32[64,112]{1,0:T(8,128)} %gate_keep.1, s32[64,112]{1,0:T(8,128)} %up_keep.1, s32[112,64]{1,0:T(8,128)} %copy.8.down_keep), custom_call_target="tpu_custom_call" | custom-call | flops 22548578304 | bytes 22020096 | tf_op jit(solution)/shard_map/pallas_call | solution.py:442
  246.5 1.9 copy.10
